TPU v7x, 32 devices: a whole 2x2x4 slice. The times are simulated.
32 devices in a mesh: lat: 4 (over z), lon: 8 (over y, x, core).
Axes of the slice: x: 2, y: 2, z: 4, core: 2. Of those that a mesh axis runs over, the one named last changes fastest.
Arguments:
- tracer: float32 [64, 3600, 128], P('lat', 'lon'), may hold values from -6 to 6
- east_courant: float32 [64, 3600, 128], P('lat', 'lon'), may hold values from -0.3 to 0.3
- east_diffusion: float32 [64, 3600, 128], P('lat', 'lon'), may hold values from 0.05 to 0.2
- south_courant: float32 [64, 3600, 128], P('lat', 'lon'), may hold values from -0.3 to 0.3
- south_diffusion: float32 [64, 3600, 128], P('lat', 'lon'), may hold values from 0.05 to 0.2
- cutoff: int32 [64], replicated, may hold values from 1 to 1800, as said below
Outputs:
- advanced: float32 [64, 3600, 128], P('lat', 'lon')
Inputs may be any that keep to these rules, and one draw needn't show every extreme that they name: Rows whose distance in rows from the nearer pole is 10 or more have cutoff 1800; all other rows have cutoffs below 1800, and the two rows at the poles have cutoff 1.
All inputs are finite; a program needn't handle non-finite values.
Results may differ from a plain program's by a relative error of at most 0.000098.
Values sent between devices are 32-bit elements; how exact they have to be, the bound alone decides.
A program may use at most 128 MiB of HBM per device.

v0:
```python
import functools
import math

import jax
import jax.numpy as jnp
import ml_dtypes
import numpy as np
from jax import lax
from jax.experimental import pallas as pl
from jax.experimental.pallas import tpu as pltpu
from jax.sharding import PartitionSpec as P

SUBSTEPS = 2


def extended(block, sides, width, periodic):
    for axis, dim in sides:
        count = lax.axis_size(axis)
        forward = [(i, i + 1) for i in range(count - 1)]
        if periodic:
            forward.append((count - 1, 0))
        backward = [(target, source) for source, target in forward]
        low = lax.ppermute(
            lax.slice_in_dim(block, block.shape[dim] - width, None, axis=dim), axis, forward
        )
        high = lax.ppermute(lax.slice_in_dim(block, 0, width, axis=dim), axis, backward)
        block = jnp.concatenate([low, block, high], axis=dim)
    return block


def advance(field, east_speed, east_mix, south_speed, south_mix):
    east_flux = east_speed[:, :-1] * 0.5 * (field[:, :-1] + field[:, 1:]) - east_mix[:, :-1] * (
        field[:, 1:] - field[:, :-1]
    )
    south_flux = south_speed[1:] * 0.5 * (field[:-1] + field[1:]) - south_mix[1:] * (
        field[1:] - field[:-1]
    )
    across = east_flux[1:-1, 1:] - east_flux[1:-1, :-1]
    meridian = south_flux[1:, 1:-1] - south_flux[:-1, 1:-1]
    return field[1:-1, 1:-1] - across - meridian


def split_four(coefs, levels):
    return (
        coefs[:, :, :levels],
        coefs[:, :, levels : 2 * levels],
        coefs[:, :, 2 * levels : 3 * levels],
        coefs[:, :, 3 * levels :],
    )


def extend(values, depth):
    beside_all = extended(values, (("lon", 1),), depth, True)
    return extended(beside_all, (("lat", 0),), depth, False)


def angles(rows, cols, length):
    first = jnp.arange(rows, dtype=jnp.int32)
    second = jnp.arange(cols, dtype=jnp.int32)
    phase = first[:, None] * second[None, :] % length
    angle = phase.astype(jnp.float32) * (2.0 * math.pi / length)
    return (jnp.cos(angle), jnp.sin(angle))


def contract(form, values, table):
    return jnp.einsum(
        form, values, table, precision=lax.Precision.HIGHEST, preferred_element_type=jnp.float32
    )


def rotate(real, imag, cosine, sine, form, sign):
    new_real = contract(form, real, cosine) - sign * contract(form, imag, sine)
    new_imag = contract(form, imag, cosine) + sign * contract(form, real, sine)
    return (new_real, new_imag)


def pick_factor(length):
    factor = 1
    for candidate in range(1, int(math.isqrt(length)) + 1):
        if length % candidate == 0:
            factor = candidate
    return factor


def filter_rows_local(whole_rows, item_cut):
    share, length, levels = whole_rows.shape
    outer = pick_factor(length)
    inner = length // outer
    shaped = whole_rows.reshape(share, outer, inner, levels)
    cos_outer, sin_outer = angles(outer, outer, outer)
    cos_inner, sin_inner = angles(inner, inner, inner)
    cos_twist, sin_twist = angles(outer, inner, length)
    first_real = contract("janl,ak->jknl", shaped, cos_outer)
    first_imag = -contract("janl,ak->jknl", shaped, sin_outer)
    twist_real = cos_twist[None, :, :, None]
    twist_imag = sin_twist[None, :, :, None]
    turned_real = first_real * twist_real + first_imag * twist_imag
    turned_imag = first_imag * twist_real - first_real * twist_imag
    spec_real, spec_imag = rotate(
        turned_real, turned_imag, cos_inner, sin_inner, "jknl,nm->jkml", -1.0
    )
    low = jnp.arange(outer, dtype=jnp.int32)
    high = jnp.arange(inner, dtype=jnp.int32)
    wave = low[:, None] + outer * high[None, :]
    folded = jnp.minimum(wave, length - wave).astype(jnp.float32)
    levelled = item_cut.astype(jnp.float32)[:, None, None]
    damping = jnp.minimum(1.0, (levelled / jnp.maximum(folded, 1.0)[None, :, :]) ** 2) / length
    spec_real = spec_real * damping[:, :, :, None]
    spec_imag = spec_imag * damping[:, :, :, None]
    back_real, back_imag = rotate(spec_real, spec_imag, cos_inner, sin_inner, "jkml,nm->jknl", 1.0)
    unturned_real = back_real * twist_real - back_imag * twist_imag
    unturned_imag = back_imag * twist_real + back_real * twist_imag
    result = contract("jknl,ak->janl", unturned_real, cos_outer) - contract(
        "jknl,ak->janl", unturned_imag, sin_outer
    )
    return result.reshape(share, length, levels)


def smooth_rows(block, global_rows, cutoff):
    whole_rows = lax.all_to_all(block, "lon", split_axis=0, concat_axis=1, tiled=True)
    share = whole_rows.shape[0]
    length = whole_rows.shape[1]
    first = lax.axis_index("lon") * share
    item_row = lax.dynamic_slice_in_dim(global_rows, first, share, 0)
    matcher = item_row[:, None] == jnp.arange(cutoff.shape[0], dtype=jnp.int32)[None, :]
    item_cut = jnp.sum(jnp.where(matcher, cutoff[None, :], 0), axis=1)
    smoothed = filter_rows_local(whole_rows, item_cut)
    kept = jnp.where((item_cut < length // 2)[:, None, None], smoothed, whole_rows)
    return lax.all_to_all(kept, "lon", split_axis=1, concat_axis=0, tiled=True)


def on_device(tracer, east_courant, east_diffusion, south_courant, south_diffusion, cutoff):
    count, width, levels = tracer.shape
    lat_pos = lax.axis_index("lat")
    rows_here = lat_pos * count + jnp.arange(count, dtype=jnp.int32)
    keeper = (rows_here > 0).astype(jnp.float32)[:, None, None]
    coefs = jnp.concatenate(
        [east_courant, east_diffusion, south_courant * keeper, south_diffusion * keeper], 2
    )
    field = tracer
    coef_ext = extend(coefs, 1)
    for substep in range(SUBSTEPS):
        field = advance(extend(field, 1), *split_four(coef_ext, levels))
    field = smooth_rows(field, rows_here, cutoff)
    return field


MESH = pl.DeviceIdType.MESH


def padded(length):
    return -(-length // 16) * 16


def split_bf16(values):
    high = values.astype(ml_dtypes.bfloat16)
    low = (values - high.astype(np.float64)).astype(ml_dtypes.bfloat16)
    return high, low


def tables(parts, width):
    tall = padded(width)
    place = np.arange(width)
    angle = (place[:, None] * place[None, :] % width) * (2.0 * np.pi / width)
    stack = np.zeros((4, tall, tall), ml_dtypes.bfloat16)
    cos_high, cos_low = split_bf16(np.cos(angle))
    sin_high, sin_low = split_bf16(np.sin(angle))
    for index, table in enumerate((cos_high, sin_high, cos_low, sin_low)):
        stack[index, :width, :width] = table
    half = parts // 2 + 1
    turn = np.arange(half)[:, None] * place[None, :] * (2.0 * np.pi / (parts * width))
    twist = np.zeros((2, half, tall, 128), np.float32)
    twist[0, :, :width] = np.cos(turn)[:, :, None]
    twist[1, :, :width] = np.sin(turn)[:, :, None]
    return stack.reshape(4 * tall, tall), twist


def block_kernel(
    rows, width, parts, bands, polar,
    cut_ref, f_in, ec_in, ed_in, sc_in, sd_in, dft_in, tw_in, out,
    f0, f1, ec, ed, sc, sd, dft, tw, whole, spec,
    to_east0, to_west0, to_east1, to_west1, from_west0, from_east0, from_west1, from_east1,
    load_sem, lon_send, lon_recv, z_send, z_recv, go_send, go_recv, back_send, back_recv, out_sem,
):
    me = lax.axis_index("lon")
    lat = lax.axis_index("lat")
    east = lax.rem(me + 1, parts)
    west = lax.rem(me + parts - 1, parts)
    has_south = lat > 0
    has_north = lat < bands - 1
    is_polar = jnp.logical_or(lat == 0, lat == bands - 1)
    base = jnp.where(lat == 0, 0, rows - polar)
    tall = padded(width)
    half = parts // 2 + 1

    loads = [
        pltpu.make_async_copy(f_in, f0.at[pl.ds(1, rows)], load_sem.at[0]),
        pltpu.make_async_copy(ec_in, ec, load_sem.at[1]),
        pltpu.make_async_copy(ed_in, ed, load_sem.at[2]),
        pltpu.make_async_copy(sc_in, sc.at[pl.ds(0, rows)], load_sem.at[3]),
        pltpu.make_async_copy(sd_in, sd.at[pl.ds(0, rows)], load_sem.at[4]),
        pltpu.make_async_copy(dft_in, dft, load_sem.at[5]),
        pltpu.make_async_copy(tw_in, tw, load_sem.at[6]),
    ]
    for load in loads:
        load.start()

    barrier = pltpu.get_barrier_semaphore()
    for step in range(1, parts):
        pl.semaphore_signal(
            barrier, 1, device_id={"lon": lax.rem(me + step, parts)}, device_id_type=MESH
        )

    @pl.when(has_south)
    def _():
        pl.semaphore_signal(barrier, 1, device_id={"lat": lat - 1}, device_id_type=MESH)

    @pl.when(has_north)
    def _():
        pl.semaphore_signal(barrier, 1, device_id={"lat": lat + 1}, device_id_type=MESH)

    peers = parts - 1 + jnp.where(has_south, 1, 0) + jnp.where(has_north, 1, 0)
    pl.semaphore_wait(barrier, peers)

    def remote(src, dst, send, recv, where):
        return pltpu.make_async_remote_copy(
            src_ref=src, dst_ref=dst, send_sem=send, recv_sem=recv,
            device_id=where, device_id_type=MESH,
        )

    north = {"lat": lax.rem(lat + 1, bands)}
    south = {"lat": lax.rem(lat + bands - 1, bands)}
    up0 = remote(f_in.at[rows - 1], f0.at[0], z_send.at[0], z_recv.at[0], north)
    down0 = [
        remote(f_in.at[0], f0.at[rows + 1], z_send.at[1], z_recv.at[1], south),
        remote(sc_in.at[0], sc.at[rows], z_send.at[2], z_recv.at[2], south),
        remote(sd_in.at[0], sd.at[rows], z_send.at[3], z_recv.at[3], south),
    ]
    up1 = remote(f1.at[rows], f1.at[0], z_send.at[4], z_recv.at[4], north)
    down1 = remote(f1.at[1], f1.at[rows + 1], z_send.at[5], z_recv.at[5], south)
    east0 = remote(to_east0, from_west0, lon_send.at[0], lon_recv.at[0], {"lon": east})
    west0 = remote(to_west0, from_east0, lon_send.at[1], lon_recv.at[1], {"lon": west})
    east1 = remote(to_east1, from_west1, lon_send.at[2], lon_recv.at[2], {"lon": east})
    west1 = remote(to_west1, from_east1, lon_send.at[3], lon_recv.at[3], {"lon": west})

    @pl.when(has_north)
    def _():
        up0.start()

    @pl.when(has_south)
    def _():
        for copy in down0:
            copy.start()

    for load in loads[:3]:
        load.wait()

    @pl.loop(0, rows)
    def _(j):
        to_east0[0, j] = f0[j + 1, width - 1 : width, :]
        to_east0[1, j] = ec[j, width - 1 : width, :]
        to_east0[2, j] = ed[j, width - 1 : width, :]
        to_west0[j] = f0[j + 1, 0:1, :]

    east0.start()
    west0.start()
    loads[3].wait()
    loads[4].wait()
    nothing = jnp.zeros((width, 128), jnp.float32)

    @pl.when(lat == 0)
    def _():
        f0[0] = nothing
        f1[0] = nothing
        sc[0] = nothing
        sd[0] = nothing

    @pl.when(lat == bands - 1)
    def _():
        f0[rows + 1] = nothing
        f1[rows + 1] = nothing
        sc[rows] = nothing
        sd[rows] = nothing

    def advance_row(src, dst, j, west_col, east_col):
        value = src[j + 1]
        beside = jnp.concatenate([value[1:], east_col[j]], axis=0)
        flux = ec[j] * 0.5 * (value + beside) - ed[j] * (beside - value)
        edge = west_col[j]
        first = value[0:1]
        entering = from_west0[1, j] * 0.5 * (edge + first) - from_west0[2, j] * (first - edge)
        flux_west = jnp.concatenate([entering, flux[:-1]], axis=0)
        below = src[j]
        above = src[j + 2]
        flux_south = sc[j] * 0.5 * (below + value) - sd[j] * (value - below)
        flux_north = sc[j + 1] * 0.5 * (value + above) - sd[j + 1] * (above - value)
        dst[j + 1] = value - (flux - flux_west) - (flux_north - flux_south)

    def wait_z0():
        @pl.when(has_south)
        def _():
            up0.wait_recv()

        @pl.when(has_north)
        def _():
            for copy in down0:
                copy.wait_recv()

    def wait_z1():
        @pl.when(has_south)
        def _():
            up1.wait_recv()

        @pl.when(has_north)
        def _():
            down1.wait_recv()

    @pl.when(jnp.logical_not(is_polar))
    def _():
        wait_z0()

    east0.wait_recv()
    west0.wait_recv()
    ascending = lat < bands // 2

    @pl.loop(0, rows)
    def _(t):
        j = jnp.where(ascending, t, rows - 1 - t)

        @pl.when(jnp.logical_and(is_polar, t == rows - 1))
        def _():
            wait_z0()

        advance_row(f0, f1, j, from_west0.at[0], from_east0)
        to_east1[j] = f1[j + 1, width - 1 : width, :]
        to_west1[j] = f1[j + 1, 0:1, :]

    east1.start()
    west1.start()

    @pl.when(has_north)
    def _():
        up1.start()

    @pl.when(has_south)
    def _():
        down1.start()

    east1.wait_recv()
    west1.wait_recv()

    def owner_of(r):
        return jnp.where(r < parts, r, (r - parts) * (parts - 1))

    def go_copy(r, j):
        slot = r // parts
        return remote(
            f0.at[j + 1], whole.at[slot, me], go_send.at[r], go_recv.at[slot, me],
            {"lon": owner_of(r)},
        )

    def go_local(r, j):
        slot = r // parts
        return pltpu.make_async_copy(f0.at[j + 1], whole.at[slot, me], go_send.at[r])

    def filter_slot(slot, r):
        for step in range(1, parts):
            source = lax.rem(me + step, parts)
            remote(
                f0.at[1], whole.at[slot, source], go_send.at[r], go_recv.at[slot, source],
                {"lon": source},
            ).wait_recv()
        go_local(r, base + r).wait()
        extra = jnp.zeros((tall - width, 128), jnp.float32)
        pieces = [whole[slot, a] for a in range(parts)]
        for q in range(half):
            real, imag = None, None
            for a in range(parts // 2):
                merged = (
                    pieces[a] + pieces[a + parts // 2] if q % 2 == 0 else pieces[a] - pieces[a + parts // 2]
                )
                turn = 2.0 * math.pi * ((a * q) % parts) / parts
                cosine, sine = math.cos(turn), math.sin(turn)
                if abs(cosine) > 1e-9:
                    term = merged if cosine > 1 - 1e-9 else merged * cosine
                    real = term if real is None else real + term
                if abs(sine) > 1e-9:
                    term = merged * (-sine)
                    imag = term if imag is None else imag + term
            real = jnp.concatenate([real, extra], axis=0)
            if imag is None:
                new_real = real * tw[0, q]
                new_imag = -real * tw[1, q]
            else:
                imag = jnp.concatenate([imag, extra], axis=0)
                new_real = real * tw[0, q] + imag * tw[1, q]
                new_imag = imag * tw[0, q] - real * tw[1, q]
            spec[q, :, 0:128] = new_real
            spec[q, :, 128:256] = new_imag

        cut = cut_ref[lat * rows + base + r].astype(jnp.float32)
        length = parts * width

        def products(values):
            high = values.astype(jnp.bfloat16)
            low = (values - high.astype(jnp.float32)).astype(jnp.bfloat16)
            main = jnp.dot(dft[...], high, preferred_element_type=jnp.float32)
            rest = jnp.dot(dft[0 : 2 * tall, :], low, preferred_element_type=jnp.float32)
            by_cos = main[0:tall] + (main[2 * tall : 3 * tall] + rest[0:tall])
            by_sin = main[tall : 2 * tall] + (main[3 * tall : 4 * tall] + rest[tall : 2 * tall])
            return by_cos, by_sin

        @pl.loop(0, half)
        def _(q):
            by_cos, by_sin = products(spec[q])
            real = by_cos[:, 0:128] + by_sin[:, 128:256]
            imag = by_cos[:, 128:256] - by_sin[:, 0:128]
            wave = q + parts * lax.broadcasted_iota(jnp.int32, (tall, 128), 0)
            folded = jnp.maximum(jnp.minimum(wave, length - wave), 1).astype(jnp.float32)
            ratio = cut / folded
            damping = jnp.minimum(1.0, ratio * ratio) * (1.0 / length)
            both = jnp.concatenate([real * damping, imag * damping], axis=1)
            by_cos, by_sin = products(both)
            real = by_cos[:, 0:128] - by_sin[:, 128:256]
            imag = by_cos[:, 128:256] + by_sin[:, 0:128]
            spec[q, :, 0:128] = real * tw[0, q] - imag * tw[1, q]
            spec[q, :, 128:256] = imag * tw[0, q] + real * tw[1, q]

        for a in range(parts):
            total = spec[0, 0:width, 0:128]
            for q in range(1, half):
                turn = 2.0 * math.pi * ((a * q) % parts) / parts
                weight = 1.0 if q == parts // 2 else 2.0
                cosine, sine = weight * math.cos(turn), weight * math.sin(turn)
                if abs(cosine) > 1e-9:
                    total = total + spec[q, 0:width, 0:128] * cosine
                if abs(sine) > 1e-9:
                    total = total - spec[q, 0:width, 128:256] * sine
            whole[slot, a] = total
        for step in range(1, parts):
            target = lax.rem(me + step, parts)
            remote(
                whole.at[slot, target], out.at[base + r], back_send.at[slot, step],
                back_recv.at[r], {"lon": target},
            ).start()
        pltpu.make_async_copy(whole.at[slot, me], out.at[base + r], back_recv.at[r]).start()

    @pl.when(is_polar)
    def _():
        @pl.loop(0, polar)
        def _(t):
            r = lax.rem(me + t, polar)
            j = base + r
            advance_row(f1, f0, j, from_west1, from_east1)

            @pl.when(owner_of(r) == me)
            def _():
                go_local(r, j).start()

            @pl.when(owner_of(r) != me)
            def _():
                go_copy(r, j).start()

        wait_z1()
        rest = jnp.where(lat == 0, polar, 0)

        @pl.loop(0, rows - polar)
        def _(t):
            advance_row(f1, f0, rest + t, from_west1, from_east1)

        keep = pltpu.make_async_copy(
            f0.at[pl.ds(rest + 1, rows - polar)], out.at[pl.ds(rest, rows - polar)], out_sem
        )
        keep.start()
        loads[5].wait()
        loads[6].wait()
        filter_slot(0, me)

        @pl.loop(parts, polar)
        def _(r):
            @pl.when(owner_of(r) == me)
            def _():
                filter_slot(1, r)

        keep.wait()

        @pl.loop(0, polar)
        def _(r):
            slot = r // parts

            @pl.when(owner_of(r) != me)
            def _():
                go_copy(r, base + r).wait_send()
                remote(
                    whole.at[slot, me], out.at[base + r], back_send.at[slot, 0],
                    back_recv.at[r], {"lon": east},
                ).wait_recv()

            @pl.when(owner_of(r) == me)
            def _():
                for step in range(1, parts):
                    target = lax.rem(me + step, parts)
                    remote(
                        whole.at[slot, target], out.at[base + r], back_send.at[slot, step],
                        back_recv.at[r], {"lon": target},
                    ).wait_send()
                pltpu.make_async_copy(
                    whole.at[slot, me], out.at[base + r], back_recv.at[r]
                ).wait()

    @pl.when(jnp.logical_not(is_polar))
    def _():
        wait_z1()

        @pl.loop(0, rows)
        def _(t):
            advance_row(f1, f0, t, from_west1, from_east1)

        keep = pltpu.make_async_copy(f0.at[pl.ds(1, rows)], out, out_sem)
        keep.start()
        loads[5].wait()
        loads[6].wait()
        keep.wait()

    for copy in (east0, west0, east1, west1):
        copy.wait_send()

    @pl.when(has_north)
    def _():
        up0.wait_send()
        up1.wait_send()

    @pl.when(has_south)
    def _():
        for copy in down0:
            copy.wait_send()
        down1.wait_send()


def on_block(mesh, polar, tracer, east_courant, east_diffusion, south_courant, south_diffusion, cutoff):
    rows, width, levels = tracer.shape
    parts, bands = mesh.shape["lon"], mesh.shape["lat"]
    tall, half = padded(width), parts // 2 + 1
    stack, twist = tables(parts, width)
    hbm = pl.BlockSpec(memory_space=pl.ANY)
    field = lambda count: pltpu.VMEM((count, width, levels), jnp.float32)
    edge = pltpu.VMEM((rows, 1, levels), jnp.float32)
    edge3 = pltpu.VMEM((3, rows, 1, levels), jnp.float32)
    slots = -(-polar // parts)
    dma = lambda *shape: pltpu.SemaphoreType.DMA(shape)
    return pl.pallas_call(
        functools.partial(block_kernel, rows, width, parts, bands, polar),
        out_shape=jax.ShapeDtypeStruct(tracer.shape, jnp.float32),
        in_specs=[pl.BlockSpec(memory_space=pltpu.SMEM)] + [hbm] * 7,
        out_specs=hbm,
        scratch_shapes=[
            field(rows + 2), field(rows + 2), field(rows), field(rows), field(rows + 1), field(rows + 1),
            pltpu.VMEM(stack.shape, jnp.bfloat16),
            pltpu.VMEM(twist.shape, jnp.float32),
            pltpu.VMEM((slots, parts, width, levels), jnp.float32),
            pltpu.VMEM((half, tall, 2 * levels), jnp.float32),
            edge3, edge, edge, edge, edge3, edge, edge, edge,
            dma(7), dma(4), dma(4), dma(6), dma(6), dma(polar), dma(slots, parts),
            dma(slots, parts), dma(polar), pltpu.SemaphoreType.DMA,
        ],
        compiler_params=pltpu.CompilerParams(
            collective_id=0, has_side_effects=True, vmem_limit_bytes=60 * 2**20
        ),
    )(
        cutoff, tracer, east_courant, east_diffusion, south_courant, south_diffusion,
        jnp.asarray(stack), jnp.asarray(twist),
    )


def solution(mesh):
    in_specs = (P("lat", "lon", None),) * 5 + (P(),)
    out_specs = P("lat", "lon", None)
    parts, bands = mesh.shape["lon"], mesh.shape["lat"]

    def run(tracer, *others):
        polar = tracer.shape[0] // 6
        rows = tracer.shape[0] // bands
        fits = (
            bands > 2
            and polar + SUBSTEPS <= rows
            and parts <= polar <= parts + 2
            and parts % 8 == 0
            and tracer.shape[2] == 128
        )
        body = functools.partial(on_block, mesh, polar) if fits else on_device
        return jax.shard_map(
            body, mesh=mesh, in_specs=in_specs, out_specs=out_specs, check_vma=False
        )(tracer, *others)

    return run
```

profile of v0, /device:TPU:7, one launch (start us, length us, event | category | flops | bytes accessed | tf_op | source)
XLA Modules:
  0.0 122.3 jit_solution(5991725612182249449)
XLA Ops:
  0.0 0.0 copy-start
  0.0 5.2 %copy.9.f_in = f32[16,450,128]{2,1,0:T(8,128)} copy(f32[16,450,128]{2,0,1:T(8,128)} %param.8) | data formatting | bytes 7372800 | tf_op args[0]
  5.2 0.0 copy-done
  5.2 0.0 copy-start.1
  5.2 3.0 %copy.10.ec_in = f32[16,450,128]{2,1,0:T(8,128)} copy(f32[16,450,128]{2,0,1:T(8,128)S(1)} %copy-done) | data formatting | bytes 7372800 | tf_op args[1]
  8.2 0.0 copy-done.1
  8.2 0.0 copy-start.2
  8.2 3.0 %copy.11.ed_in = f32[16,450,128]{2,1,0:T(8,128)} copy(f32[16,450,128]{2,0,1:T(8,128)S(1)} %copy-done.1) | data formatting | bytes 7372800 | tf_op args[2]
  11.2 0.0 copy-done.2
  11.2 0.0 copy-start.3
  11.2 3.1 %copy.12.sc_in = f32[16,450,128]{2,1,0:T(8,128)} copy(f32[16,450,128]{2,0,1:T(8,128)S(1)} %copy-done.2) | data formatting | bytes 7372800 | tf_op args[3]
  14.3 0.0 copy-done.3
  14.3 2.9 %copy.13.sd_in = f32[16,450,128]{2,1,0:T(8,128)} copy(f32[16,450,128]{2,0,1:T(8,128)S(1)} %copy-done.3) | data formatting | bytes 7372800 | tf_op args[4]
  17.2 100.5 %shard_map.82 = f32[16,450,128]{2,1,0:T(8,128)} custom-call(s32[64]{0:T(128)} %cut_ref.1, f32[16,450,128]{2,1,0:T(8,128)} %copy.9.f_in, f32[16,450,128]{2,1,0:T(8,128)} %copy.10.ec_in, f32[16,450,128]{2,1,0:T(8,128)} %copy.11.ed_in, f32[16,450,128]{2,1,0:T(8,128)} %copy.12.sc_in, f32[16,450,128]{2,1,0:T(8,128)} %copy.13.sd_in, ...), custom_call_target="tpu_custom_call" | custom-call | tf_op jit(solution)/shard_map/pallas_call | solution.py:551
  117.7 4.6 %copy.14 = f32[16,450,128]{2,0,1:T(8,128)} copy(f32[16,450,128]{2,1,0:T(8,128)} %shard_map.82) | data formatting | bytes 7372800 | tf_op jit(solution)/shard_map/pallas_call | solution.py:551
Async XLA Ops:
  0.0 5.2 %copy-start = (f32[16,450,128]{2,0,1:T(8,128)S(1)}, f32[16,450,128]{2,0,1:T(8,128)}, u32[]{:S(2)}) copy-start(f32[16,450,128]{2,0,1:T(8,128)} %param.9) | copy-start | bytes 11059204
  5.2 3.0 %copy-start.1 = (f32[16,450,128]{2,0,1:T(8,128)S(1)}, f32[16,450,128]{2,0,1:T(8,128)}, u32[]{:S(2)}) copy-start(f32[16,450,128]{2,0,1:T(8,128)} %param.10) | copy-start | bytes 11059204
  8.2 3.1 %copy-start.2 = (f32[16,450,128]{2,0,1:T(8,128)S(1)}, f32[16,450,128]{2,0,1:T(8,128)}, u32[]{:S(2)}) copy-start(f32[16,450,128]{2,0,1:T(8,128)} %param.11) | copy-start | bytes 11059204
  11.2 3.1 %copy-start.3 = (f32[16,450,128]{2,0,1:T(8,128)S(1)}, f32[16,450,128]{2,0,1:T(8,128)}, u32[]{:S(2)}) copy-start(f32[16,450,128]{2,0,1:T(8,128)} %param.12) | copy-start | bytes 11059204
where the time goes:
time: 123 us; the launch traced here: 122 us
  Pallas kernels  100 us (81%)
  local copies, waits for them, and re-layouts  21.8 us (18%)
    pallas_call x1, Pallas kernels, on_block(): pl.pallas_call(functools.partial(block_kernel, rows, width, parts, bands,...  100 us
    unnamed x13, local copies, waits for them, and re-layouts  17.2 us
    pallas_call x1, local copies, waits for them, and re-layouts, on_block(): pl.pallas_call(functools.partial(block_kernel, rows, width, parts, bands,...  4.61 us

commit v1 on v0

--- a/solution.py
+++ b/solution.py
@@ -179,8 +179,8 @@
     rows, width, parts, bands, polar,
     cut_ref, f_in, ec_in, ed_in, sc_in, sd_in, dft_in, tw_in, out,
     f0, f1, ec, ed, sc, sd, dft, tw, whole, spec,
-    to_east0, to_west0, to_east1, to_west1, from_west0, from_east0, from_west1, from_east1,
-    load_sem, lon_send, lon_recv, z_send, z_recv, go_send, go_recv, back_send, back_recv, out_sem,
+    to_east1, to_west1, from_west0, from_east0, from_west1, from_east1,
+    load_sem, table_sem, lon_send, lon_recv, z_send, z_recv, go_send, go_recv, back_send, back_recv, out_sem,
 ):
     me = lax.axis_index("lon")
     lat = lax.axis_index("lat")
@@ -193,16 +193,29 @@
     tall = padded(width)
     half = parts // 2 + 1
 
-    loads = [
-        pltpu.make_async_copy(f_in, f0.at[pl.ds(1, rows)], load_sem.at[0]),
-        pltpu.make_async_copy(ec_in, ec, load_sem.at[1]),
-        pltpu.make_async_copy(ed_in, ed, load_sem.at[2]),
-        pltpu.make_async_copy(sc_in, sc.at[pl.ds(0, rows)], load_sem.at[3]),
-        pltpu.make_async_copy(sd_in, sd.at[pl.ds(0, rows)], load_sem.at[4]),
-        pltpu.make_async_copy(dft_in, dft, load_sem.at[5]),
-        pltpu.make_async_copy(tw_in, tw, load_sem.at[6]),
+    ascending = lat < bands // 2
+
+    def place(t):
+        return jnp.where(ascending, t, rows - 1 - t)
+
+    def load_row(j):
+        return [
+            pltpu.make_async_copy(src.at[:, j, :], dst.at[j + shift], load_sem.at[index, j])
+            for index, (src, dst, shift) in enumerate(
+                ((f_in, f0, 1), (ec_in, ec, 0), (ed_in, ed, 0), (sc_in, sc, 0), (sd_in, sd, 0))
+            )
+        ]
+
+    @pl.loop(0, rows)
+    def _(t):
+        for load in load_row(place(t)):
+            load.start()
+
+    table_loads = [
+        pltpu.make_async_copy(dft_in, dft, table_sem.at[0]),
+        pltpu.make_async_copy(tw_in, tw, table_sem.at[1]),
     ]
-    for load in loads:
+    for load in table_loads:
         load.start()
 
     barrier = pltpu.get_barrier_semaphore()
@@ -230,19 +243,26 @@
 
     north = {"lat": lax.rem(lat + 1, bands)}
     south = {"lat": lax.rem(lat + bands - 1, bands)}
-    up0 = remote(f_in.at[rows - 1], f0.at[0], z_send.at[0], z_recv.at[0], north)
+    up0 = remote(f_in.at[:, rows - 1, :], f0.at[0], z_send.at[0], z_recv.at[0], north)
     down0 = [
-        remote(f_in.at[0], f0.at[rows + 1], z_send.at[1], z_recv.at[1], south),
-        remote(sc_in.at[0], sc.at[rows], z_send.at[2], z_recv.at[2], south),
-        remote(sd_in.at[0], sd.at[rows], z_send.at[3], z_recv.at[3], south),
+        remote(f_in.at[:, 0, :], f0.at[rows + 1], z_send.at[1], z_recv.at[1], south),
+        remote(sc_in.at[:, 0, :], sc.at[rows], z_send.at[2], z_recv.at[2], south),
+        remote(sd_in.at[:, 0, :], sd.at[rows], z_send.at[3], z_recv.at[3], south),
     ]
     up1 = remote(f1.at[rows], f1.at[0], z_send.at[4], z_recv.at[4], north)
     down1 = remote(f1.at[1], f1.at[rows + 1], z_send.at[5], z_recv.at[5], south)
-    east0 = remote(to_east0, from_west0, lon_send.at[0], lon_recv.at[0], {"lon": east})
-    west0 = remote(to_west0, from_east0, lon_send.at[1], lon_recv.at[1], {"lon": west})
+    edges0 = [
+        remote(f_in.at[width - 1], from_west0.at[0], lon_send.at[0], lon_recv.at[0], {"lon": east}),
+        remote(ec_in.at[width - 1], from_west0.at[1], lon_send.at[1], lon_recv.at[1], {"lon": east}),
+        remote(ed_in.at[width - 1], from_west0.at[2], lon_send.at[4], lon_recv.at[4], {"lon": east}),
+        remote(f_in.at[0], from_east0, lon_send.at[5], lon_recv.at[5], {"lon": west}),
+    ]
     east1 = remote(to_east1, from_west1, lon_send.at[2], lon_recv.at[2], {"lon": east})
     west1 = remote(to_west1, from_east1, lon_send.at[3], lon_recv.at[3], {"lon": west})
 
+    for copy in edges0:
+        copy.start()
+
     @pl.when(has_north)
     def _():
         up0.start()
@@ -252,20 +272,8 @@
         for copy in down0:
             copy.start()
 
-    for load in loads[:3]:
+    for load in load_row(place(0)):
         load.wait()
-
-    @pl.loop(0, rows)
-    def _(j):
-        to_east0[0, j] = f0[j + 1, width - 1 : width, :]
-        to_east0[1, j] = ec[j, width - 1 : width, :]
-        to_east0[2, j] = ed[j, width - 1 : width, :]
-        to_west0[j] = f0[j + 1, 0:1, :]
-
-    east0.start()
-    west0.start()
-    loads[3].wait()
-    loads[4].wait()
     nothing = jnp.zeros((width, 128), jnp.float32)
 
     @pl.when(lat == 0)
@@ -284,11 +292,11 @@
 
     def advance_row(src, dst, j, west_col, east_col):
         value = src[j + 1]
-        beside = jnp.concatenate([value[1:], east_col[j]], axis=0)
+        beside = jnp.concatenate([value[1:], east_col[pl.ds(j, 1), :]], axis=0)
         flux = ec[j] * 0.5 * (value + beside) - ed[j] * (beside - value)
-        edge = west_col[j]
+        edge = west_col[pl.ds(j, 1), :]
         first = value[0:1]
-        entering = from_west0[1, j] * 0.5 * (edge + first) - from_west0[2, j] * (first - edge)
+        entering = from_west0[1, pl.ds(j, 1), :] * 0.5 * (edge + first) - from_west0[2, pl.ds(j, 1), :] * (first - edge)
         flux_west = jnp.concatenate([entering, flux[:-1]], axis=0)
         below = src[j]
         above = src[j + 2]
@@ -319,21 +327,25 @@
     def _():
         wait_z0()
 
-    east0.wait_recv()
-    west0.wait_recv()
-    ascending = lat < bands // 2
+    for copy in edges0:
+        copy.wait_recv()
 
     @pl.loop(0, rows)
     def _(t):
-        j = jnp.where(ascending, t, rows - 1 - t)
+        j = place(t)
+
+        @pl.when(t < rows - 1)
+        def _():
+            for load in load_row(place(t + 1)):
+                load.wait()
 
         @pl.when(jnp.logical_and(is_polar, t == rows - 1))
         def _():
             wait_z0()
 
         advance_row(f0, f1, j, from_west0.at[0], from_east0)
-        to_east1[j] = f1[j + 1, width - 1 : width, :]
-        to_west1[j] = f1[j + 1, 0:1, :]
+        to_east1[pl.ds(j, 1), :] = f1[j + 1, width - 1 : width, :]
+        to_west1[pl.ds(j, 1), :] = f1[j + 1, 0:1, :]
 
     east1.start()
     west1.start()
@@ -348,6 +360,9 @@
 
     east1.wait_recv()
     west1.wait_recv()
+
+    def keep_row(j):
+        return pltpu.make_async_copy(f0.at[j + 1], out.at[:, j, :], out_sem.at[j])
 
     def owner_of(r):
         return jnp.where(r < parts, r, (r - parts) * (parts - 1))
@@ -440,10 +455,10 @@
         for step in range(1, parts):
             target = lax.rem(me + step, parts)
             remote(
-                whole.at[slot, target], out.at[base + r], back_send.at[slot, step],
+                whole.at[slot, target], out.at[:, base + r, :], back_send.at[slot, step],
                 back_recv.at[r], {"lon": target},
             ).start()
-        pltpu.make_async_copy(whole.at[slot, me], out.at[base + r], back_recv.at[r]).start()
+        pltpu.make_async_copy(whole.at[slot, me], out.at[:, base + r, :], back_recv.at[r]).start()
 
     @pl.when(is_polar)
     def _():
@@ -467,13 +482,10 @@
         @pl.loop(0, rows - polar)
         def _(t):
             advance_row(f1, f0, rest + t, from_west1, from_east1)
-
-        keep = pltpu.make_async_copy(
-            f0.at[pl.ds(rest + 1, rows - polar)], out.at[pl.ds(rest, rows - polar)], out_sem
-        )
-        keep.start()
-        loads[5].wait()
-        loads[6].wait()
+            keep_row(rest + t).start()
+
+        for load in table_loads:
+            load.wait()
         filter_slot(0, me)
 
         @pl.loop(parts, polar)
@@ -482,7 +494,9 @@
             def _():
                 filter_slot(1, r)
 
-        keep.wait()
+        @pl.loop(0, rows - polar)
+        def _(t):
+            keep_row(rest + t).wait()
 
         @pl.loop(0, polar)
         def _(r):
@@ -492,7 +506,7 @@
             def _():
                 go_copy(r, base + r).wait_send()
                 remote(
-                    whole.at[slot, me], out.at[base + r], back_send.at[slot, 0],
+                    whole.at[slot, me], out.at[:, base + r, :], back_send.at[slot, 0],
                     back_recv.at[r], {"lon": east},
                 ).wait_recv()
 
@@ -501,11 +515,11 @@
                 for step in range(1, parts):
                     target = lax.rem(me + step, parts)
                     remote(
-                        whole.at[slot, target], out.at[base + r], back_send.at[slot, step],
+                        whole.at[slot, target], out.at[:, base + r, :], back_send.at[slot, step],
                         back_recv.at[r], {"lon": target},
                     ).wait_send()
                 pltpu.make_async_copy(
-                    whole.at[slot, me], out.at[base + r], back_recv.at[r]
+                    whole.at[slot, me], out.at[:, base + r, :], back_recv.at[r]
                 ).wait()
 
     @pl.when(jnp.logical_not(is_polar))
@@ -515,14 +529,16 @@
         @pl.loop(0, rows)
         def _(t):
             advance_row(f1, f0, t, from_west1, from_east1)
-
-        keep = pltpu.make_async_copy(f0.at[pl.ds(1, rows)], out, out_sem)
-        keep.start()
-        loads[5].wait()
-        loads[6].wait()
-        keep.wait()
-
-    for copy in (east0, west0, east1, west1):
+            keep_row(t).start()
+
+        for load in table_loads:
+            load.wait()
+
+        @pl.loop(0, rows)
+        def _(t):
+            keep_row(t).wait()
+
+    for copy in edges0 + [east1, west1]:
         copy.wait_send()
 
     @pl.when(has_north)
@@ -544,13 +560,14 @@
     stack, twist = tables(parts, width)
     hbm = pl.BlockSpec(memory_space=pl.ANY)
     field = lambda count: pltpu.VMEM((count, width, levels), jnp.float32)
-    edge = pltpu.VMEM((rows, 1, levels), jnp.float32)
-    edge3 = pltpu.VMEM((3, rows, 1, levels), jnp.float32)
+    edge = pltpu.VMEM((rows, levels), jnp.float32)
+    edge3 = pltpu.VMEM((3, rows, levels), jnp.float32)
     slots = -(-polar // parts)
     dma = lambda *shape: pltpu.SemaphoreType.DMA(shape)
-    return pl.pallas_call(
+    swapped = lambda values: jnp.transpose(values, (1, 0, 2))
+    result = pl.pallas_call(
         functools.partial(block_kernel, rows, width, parts, bands, polar),
-        out_shape=jax.ShapeDtypeStruct(tracer.shape, jnp.float32),
+        out_shape=jax.ShapeDtypeStruct((width, rows, levels), jnp.float32),
         in_specs=[pl.BlockSpec(memory_space=pltpu.SMEM)] + [hbm] * 7,
         out_specs=hbm,
         scratch_shapes=[
@@ -559,17 +576,18 @@
             pltpu.VMEM(twist.shape, jnp.float32),
             pltpu.VMEM((slots, parts, width, levels), jnp.float32),
             pltpu.VMEM((half, tall, 2 * levels), jnp.float32),
-            edge3, edge, edge, edge, edge3, edge, edge, edge,
-            dma(7), dma(4), dma(4), dma(6), dma(6), dma(polar), dma(slots, parts),
-            dma(slots, parts), dma(polar), pltpu.SemaphoreType.DMA,
+            edge, edge, edge3, edge, edge, edge,
+            dma(5, rows), dma(2), dma(6), dma(6), dma(6), dma(6), dma(polar), dma(slots, parts),
+            dma(slots, parts), dma(polar), dma(rows),
         ],
         compiler_params=pltpu.CompilerParams(
             collective_id=0, has_side_effects=True, vmem_limit_bytes=60 * 2**20
         ),
     )(
-        cutoff, tracer, east_courant, east_diffusion, south_courant, south_diffusion,
-        jnp.asarray(stack), jnp.asarray(twist),
-    )
+        cutoff, swapped(tracer), swapped(east_courant), swapped(east_diffusion),
+        swapped(south_courant), swapped(south_diffusion), jnp.asarray(stack), jnp.asarray(twist),
+    )
+    return swapped(result)
 
 
 def solution(mesh):

time: 123 us -> 106 us (0.86)
  local copies, waits for them, and re-layouts: 21.8 us -> 4.12 us
  Pallas kernels: 100 us -> 102 us
    unnamed x13 -> x1, local copies, waits for them, and re-layouts: 17.2 us -> 4.12 us
    pallas_call x1 -> x0, local copies, waits for them, and re-layouts: 4.61 us -> none  [on_block(): pl.pallas_call(functools.partial(block_kernel, rows, width, parts, bands,...]
where the time goes in v1:
time: 106 us
  Pallas kernels  102 us (96%)
  local copies, waits for them, and re-layouts  4.12 us (4%)
    pallas_call x1, Pallas kernels, on_block(): pl.pallas_call(functools.partial(block_kernel, rows, width, parts, bands,...  102 us
    unnamed x1, local copies, waits for them, and re-layouts  4.12 us

profile of v1, /device:TPU:7, one launch (start us, length us, event | category | flops | bytes accessed | tf_op | source)
XLA Modules:
  0.0 105.8 jit_solution(8468730663165668291)
XLA Ops:
  0.0 101.6 %shard_map.82 = f32[450,16,128]{2,1,0:T(8,128)} custom-call(s32[64]{0:T(128)} %cut_ref.1, f32[450,16,128]{2,1,0:T(8,128)} %bitcast.7, f32[450,16,128]{2,1,0:T(8,128)} %bitcast.8, f32[450,16,128]{2,1,0:T(8,128)} %bitcast.9, f32[450,16,128]{2,1,0:T(8,128)} %bitcast.10, f32[450,16,128]{2,1,0:T(8,128)} %bitcast.11, bf16[1856,464]{1,0:T(8,128)(2,1)} %constant.4.clone.dft_in, ...), custom_call_target="tpu_custom_call" | custom-call | tf_op jit(solution)/shard_map/pallas_call | solution.py:568
  101.6 4.1 %copy.10 = f32[16,450,128]{2,0,1:T(8,128)} copy(f32[16,450,128]{2,0,1:T(8,128)} %bitcast.6) | data formatting | bytes 7372800

commit v2 on v1

--- a/solution.py
+++ b/solution.py
@@ -176,11 +176,13 @@
 
 
 def block_kernel(
-    rows, width, parts, bands, polar,
+    rows, width, parts, bands, polar, kept_owner, lent_owner,
     cut_ref, f_in, ec_in, ed_in, sc_in, sd_in, dft_in, tw_in, out,
-    f0, f1, ec, ed, sc, sd, dft, tw, whole, spec,
+    f0, f1, ec, ed, sc, sd, dft, tw, whole, spec, lent, lent_back,
     to_east1, to_west1, from_west0, from_east0, from_west1, from_east1,
-    load_sem, table_sem, lon_send, lon_recv, z_send, z_recv, go_send, go_recv, back_send, back_recv, out_sem,
+    to_east2, to_west2, from_west2, from_east2,
+    load_sem, table_sem, lon_send, lon_recv, z_send, z_recv, go_send, go_recv, back_send, back_recv,
+    lend_send, lend_recv, ret_send, ret_recv, out_sem,
 ):
     me = lax.axis_index("lon")
     lat = lax.axis_index("lat")
@@ -189,11 +191,14 @@
     has_south = lat > 0
     has_north = lat < bands - 1
     is_polar = jnp.logical_or(lat == 0, lat == bands - 1)
-    base = jnp.where(lat == 0, 0, rows - polar)
+    kept, borrowed = len(kept_owner), len(lent_owner)
+    ascending = lat < bands // 2
+    base = jnp.where(ascending, 0, rows - polar)
+    pole_lat = jnp.where(ascending, 0, bands - 1)
+    helper_lat = jnp.where(ascending, 1, bands - 2)
+    early = polar + 1
     tall = padded(width)
     half = parts // 2 + 1
-
-    ascending = lat < bands // 2
 
     def place(t):
         return jnp.where(ascending, t, rows - 1 - t)
@@ -257,8 +262,14 @@
         remote(ed_in.at[width - 1], from_west0.at[2], lon_send.at[4], lon_recv.at[4], {"lon": east}),
         remote(f_in.at[0], from_east0, lon_send.at[5], lon_recv.at[5], {"lon": west}),
     ]
-    east1 = remote(to_east1, from_west1, lon_send.at[2], lon_recv.at[2], {"lon": east})
-    west1 = remote(to_west1, from_east1, lon_send.at[3], lon_recv.at[3], {"lon": west})
+    edges1 = [
+        remote(to_east1, from_west1, lon_send.at[2], lon_recv.at[2], {"lon": east}),
+        remote(to_west1, from_east1, lon_send.at[3], lon_recv.at[3], {"lon": west}),
+    ]
+    edges2 = [
+        remote(to_east2, from_west2, lon_send.at[6], lon_recv.at[6], {"lon": east}),
+        remote(to_west2, from_east2, lon_send.at[7], lon_recv.at[7], {"lon": west}),
+    ]
 
     for copy in edges0:
         copy.start()
@@ -290,11 +301,10 @@
         sc[rows] = nothing
         sd[rows] = nothing
 
-    def advance_row(src, dst, j, west_col, east_col):
+    def advance_row(src, dst, j, edge, beyond):
         value = src[j + 1]
-        beside = jnp.concatenate([value[1:], east_col[pl.ds(j, 1), :]], axis=0)
+        beside = jnp.concatenate([value[1:], beyond], axis=0)
         flux = ec[j] * 0.5 * (value + beside) - ed[j] * (beside - value)
-        edge = west_col[pl.ds(j, 1), :]
         first = value[0:1]
         entering = from_west0[1, pl.ds(j, 1), :] * 0.5 * (edge + first) - from_west0[2, pl.ds(j, 1), :] * (first - edge)
         flux_west = jnp.concatenate([entering, flux[:-1]], axis=0)
@@ -314,12 +324,12 @@
             for copy in down0:
                 copy.wait_recv()
 
-    def wait_z1():
-        @pl.when(has_south)
+    def wait_z1(from_south):
+        @pl.when(from_south)
         def _():
             up1.wait_recv()
 
-        @pl.when(has_north)
+        @pl.when(jnp.logical_not(from_south))
         def _():
             down1.wait_recv()
 
@@ -330,64 +340,70 @@
     for copy in edges0:
         copy.wait_recv()
 
-    @pl.loop(0, rows)
-    def _(t):
-        j = place(t)
-
-        @pl.when(t < rows - 1)
-        def _():
-            for load in load_row(place(t + 1)):
-                load.wait()
-
-        @pl.when(jnp.logical_and(is_polar, t == rows - 1))
-        def _():
-            wait_z0()
-
-        advance_row(f0, f1, j, from_west0.at[0], from_east0)
-        to_east1[pl.ds(j, 1), :] = f1[j + 1, width - 1 : width, :]
-        to_west1[pl.ds(j, 1), :] = f1[j + 1, 0:1, :]
-
-    east1.start()
-    west1.start()
-
-    @pl.when(has_north)
-    def _():
-        up1.start()
-
-    @pl.when(has_south)
-    def _():
-        down1.start()
-
-    east1.wait_recv()
-    west1.wait_recv()
+    def first_substep(start, stop, east_edge, west_edge):
+        @pl.loop(start, stop)
+        def _(t):
+            j = place(t)
+
+            @pl.when(t < rows - 1)
+            def _():
+                for load in load_row(place(t + 1)):
+                    load.wait()
+
+            advance_row(f0, f1, j, from_west0[0, pl.ds(j, 1), :], from_east0[pl.ds(j, 1), :])
+            east_edge[pl.ds(t - start, 1), :] = f1[j + 1, width - 1 : width, :]
+            west_edge[pl.ds(t - start, 1), :] = f1[j + 1, 0:1, :]
+
+    def finish_first():
+        first_substep(early, rows, to_east2, to_west2)
+        for copy in edges2:
+            copy.start()
+
+        @pl.when(has_north)
+        def _():
+            up1.start()
+
+        @pl.when(has_south)
+        def _():
+            down1.start()
+
+    def second_early(t):
+        advance_row(f1, f0, place(t), from_west1[pl.ds(t, 1), :], from_east1[pl.ds(t, 1), :])
+
+    def second_late(t):
+        late = t - early
+        advance_row(f1, f0, place(t), from_west2[pl.ds(late, 1), :], from_east2[pl.ds(late, 1), :])
+
+    first_substep(0, early, to_east1, to_west1)
+    for copy in edges1:
+        copy.start()
 
     def keep_row(j):
         return pltpu.make_async_copy(f0.at[j + 1], out.at[:, j, :], out_sem.at[j])
 
-    def owner_of(r):
-        return jnp.where(r < parts, r, (r - parts) * (parts - 1))
-
-    def go_copy(r, j):
-        slot = r // parts
-        return remote(
-            f0.at[j + 1], whole.at[slot, me], go_send.at[r], go_recv.at[slot, me],
-            {"lon": owner_of(r)},
-        )
-
-    def go_local(r, j):
-        slot = r // parts
-        return pltpu.make_async_copy(f0.at[j + 1], whole.at[slot, me], go_send.at[r])
-
-    def filter_slot(slot, r):
+    def pick(table, index):
+        value = table[0]
+        for position in range(1, len(table)):
+            value = jnp.where(index == position, table[position], value)
+        return value
+
+    def send_piece(src, index, owner):
+        @pl.when(owner == me)
+        def _():
+            pltpu.make_async_copy(src, whole.at[me], go_send.at[index]).start()
+
+        @pl.when(owner != me)
+        def _():
+            remote(src, whole.at[me], go_send.at[index], go_recv.at[me], {"lon": owner}).start()
+
+    def filter_row(r):
         for step in range(1, parts):
             source = lax.rem(me + step, parts)
             remote(
-                f0.at[1], whole.at[slot, source], go_send.at[r], go_recv.at[slot, source],
-                {"lon": source},
+                f0.at[1], whole.at[source], go_send.at[0], go_recv.at[source], {"lon": source}
             ).wait_recv()
-        go_local(r, base + r).wait()
         extra = jnp.zeros((tall - width, 128), jnp.float32)
-        pieces = [whole[slot, a] for a in range(parts)]
+        pieces = [whole[a] for a in range(parts)]
         for q in range(half):
             real, imag = None, None
             for a in range(parts // 2):
@@ -413,7 +429,7 @@
             spec[q, :, 0:128] = new_real
             spec[q, :, 128:256] = new_imag
 
-        cut = cut_ref[lat * rows + base + r].astype(jnp.float32)
+        cut = cut_ref[pole_lat * rows + base + r].astype(jnp.float32)
         length = parts * width
 
         def products(values):
@@ -451,94 +467,177 @@
                     total = total + spec[q, 0:width, 0:128] * cosine
                 if abs(sine) > 1e-9:
                     total = total - spec[q, 0:width, 128:256] * sine
-            whole[slot, a] = total
-        for step in range(1, parts):
-            target = lax.rem(me + step, parts)
+            whole[a] = total
+
+    def run_owner(owners, index_of, row_of, landing):
+        for index, owner in enumerate(owners):
+            @pl.when(owner == me)
+            def _():
+                pltpu.make_async_copy(f0.at[1], whole.at[me], go_send.at[index]).wait()
+
+        owned = functools.reduce(jnp.logical_or, [owner == me for owner in owners])
+
+        @pl.when(owned)
+        def _():
+            index = index_of(me)
+            filter_row(row_of(index))
+            for step in range(1, parts):
+                target = lax.rem(me + step, parts)
+                remote(
+                    whole.at[target], landing(index), back_send.at[step], back_recv.at[index],
+                    {"lon": target},
+                ).start()
+            pltpu.make_async_copy(whole.at[me], landing(index), back_recv.at[index]).start()
+
+    def finish_owner(owners, landing):
+        owned = functools.reduce(jnp.logical_or, [owner == me for owner in owners])
+
+        @pl.when(owned)
+        def _():
+            for step in range(1, parts):
+                target = lax.rem(me + step, parts)
+                remote(
+                    whole.at[target], landing(0), back_send.at[step], back_recv.at[0],
+                    {"lon": target},
+                ).wait_send()
+
+    def wait_back(index, owner, landing):
+        @pl.when(owner == me)
+        def _():
+            pltpu.make_async_copy(whole.at[me], landing(index), back_recv.at[index]).wait()
+
+        @pl.when(owner != me)
+        def _():
             remote(
-                whole.at[slot, target], out.at[:, base + r, :], back_send.at[slot, step],
-                back_recv.at[r], {"lon": target},
-            ).start()
-        pltpu.make_async_copy(whole.at[slot, me], out.at[:, base + r, :], back_recv.at[r]).start()
+                whole.at[me], landing(index), back_send.at[0], back_recv.at[index], {"lon": east}
+            ).wait_recv()
+
+    def wait_sent(index, owner, src):
+        @pl.when(owner != me)
+        def _():
+            remote(src, whole.at[me], go_send.at[index], go_recv.at[me], {"lon": owner}).wait_send()
+
+    def inverse(owners):
+        table = [owners.index(device) if device in owners else 0 for device in range(parts)]
+        return functools.partial(pick, table)
+
+    def lend(m):
+        j = base + kept + m
+        return remote(f0.at[j + 1], lent.at[m], lend_send.at[m], lend_recv.at[m], {"lat": helper_lat})
+
+    def give_back(m):
+        return remote(
+            lent_back.at[m], out.at[:, base + kept + m, :], ret_send.at[m], ret_recv.at[m],
+            {"lat": pole_lat},
+        )
+
+    def kept_landing(r):
+        return out.at[:, base + r, :]
+
+    def lent_landing(m):
+        return lent_back.at[m]
 
     @pl.when(is_polar)
     def _():
+        for copy in edges1:
+            copy.wait_recv()
+
         @pl.loop(0, polar)
+        def _(step):
+            r = jnp.where(step < borrowed, kept + step, lax.rem(me + step - borrowed, kept))
+            second_early(place(base + r))
+
+            @pl.when(step < borrowed)
+            def _():
+                lend(step).start()
+
+            @pl.when(step >= borrowed)
+            def _():
+                send_piece(f0.at[base + r + 1], r, pick(kept_owner, r))
+
+        wait_z0()
+        finish_first()
+        second_early(polar)
+        keep_row(place(polar)).start()
+        wait_z1(lat > 0)
+        for copy in edges2:
+            copy.wait_recv()
+
+        @pl.loop(early, rows)
         def _(t):
-            r = lax.rem(me + t, polar)
-            j = base + r
-            advance_row(f1, f0, j, from_west1, from_east1)
-
-            @pl.when(owner_of(r) == me)
-            def _():
-                go_local(r, j).start()
-
-            @pl.when(owner_of(r) != me)
-            def _():
-                go_copy(r, j).start()
-
-        wait_z1()
-        rest = jnp.where(lat == 0, polar, 0)
-
-        @pl.loop(0, rows - polar)
-        def _(t):
-            advance_row(f1, f0, rest + t, from_west1, from_east1)
-            keep_row(rest + t).start()
+            second_late(t)
+            keep_row(place(t)).start()
 
         for load in table_loads:
             load.wait()
-        filter_slot(0, me)
-
-        @pl.loop(parts, polar)
+        run_owner(kept_owner, inverse(kept_owner), lambda r: r, kept_landing)
+
+        @pl.loop(polar, rows)
+        def _(t):
+            keep_row(place(t)).wait()
+
+        @pl.loop(0, kept)
         def _(r):
-            @pl.when(owner_of(r) == me)
+            wait_sent(r, pick(kept_owner, r), f0.at[1])
+            wait_back(r, pick(kept_owner, r), kept_landing)
+
+        finish_owner(kept_owner, kept_landing)
+
+        @pl.loop(0, borrowed)
+        def _(m):
+            lend(m).wait_send()
+            give_back(m).wait_recv()
+
+    @pl.when(jnp.logical_not(is_polar))
+    def _():
+        finish_first()
+        for copy in edges1 + edges2:
+            copy.wait_recv()
+        wait_z1(jnp.logical_not(ascending))
+
+        @pl.loop(0, rows - 1)
+        def _(step):
+            t = rows - 1 - step
+
+            @pl.when(t >= early)
             def _():
-                filter_slot(1, r)
-
-        @pl.loop(0, rows - polar)
-        def _(t):
-            keep_row(rest + t).wait()
-
-        @pl.loop(0, polar)
-        def _(r):
-            slot = r // parts
-
-            @pl.when(owner_of(r) != me)
+                second_late(t)
+
+            @pl.when(t < early)
             def _():
-                go_copy(r, base + r).wait_send()
-                remote(
-                    whole.at[slot, me], out.at[:, base + r, :], back_send.at[slot, 0],
-                    back_recv.at[r], {"lon": east},
-                ).wait_recv()
-
-            @pl.when(owner_of(r) == me)
-            def _():
-                for step in range(1, parts):
-                    target = lax.rem(me + step, parts)
-                    remote(
-                        whole.at[slot, target], out.at[:, base + r, :], back_send.at[slot, step],
-                        back_recv.at[r], {"lon": target},
-                    ).wait_send()
-                pltpu.make_async_copy(
-                    whole.at[slot, me], out.at[:, base + r, :], back_recv.at[r]
-                ).wait()
-
-    @pl.when(jnp.logical_not(is_polar))
-    def _():
-        wait_z1()
-
-        @pl.loop(0, rows)
-        def _(t):
-            advance_row(f1, f0, t, from_west1, from_east1)
-            keep_row(t).start()
-
+                second_early(t)
+
+            keep_row(place(t)).start()
+            for m in range(borrowed):
+                @pl.when(step == 5 + 3 * m)
+                def _():
+                    lend(m).wait_recv()
+                    send_piece(lent.at[m], m, lent_owner[m])
+
+        wait_z1(ascending)
+        second_early(0)
+        keep_row(place(0)).start()
         for load in table_loads:
             load.wait()
+        run_owner(lent_owner, inverse(lent_owner), lambda m: kept + m, lent_landing)
+
+        @pl.loop(0, borrowed)
+        def _(m):
+            wait_back(m, pick(lent_owner, m), lent_landing)
+            give_back(m).start()
 
         @pl.loop(0, rows)
         def _(t):
             keep_row(t).wait()
 
-    for copy in edges0 + [east1, west1]:
+        @pl.loop(0, borrowed)
+        def _(m):
+            wait_sent(m, pick(lent_owner, m), lent.at[m])
+            give_back(m).wait_send()
+
+        finish_owner(lent_owner, lent_landing)
+
+    for copy in edges0 + edges1 + edges2:
         copy.wait_send()
 
     @pl.when(has_north)
@@ -551,6 +650,11 @@
         for copy in down0:
             copy.wait_send()
         down1.wait_send()
+
+
+def share_rows(polar):
+    lent = 2 * polar // 5
+    return (0, 7, 2, 4, 1, 6, 3, 5)[: polar - lent], (0, 2, 4, 6, 1, 3, 5, 7)[:lent]
 
 
 def on_block(mesh, polar, tracer, east_courant, east_diffusion, south_courant, south_diffusion, cutoff):
@@ -562,11 +666,14 @@
     field = lambda count: pltpu.VMEM((count, width, levels), jnp.float32)
     edge = pltpu.VMEM((rows, levels), jnp.float32)
     edge3 = pltpu.VMEM((3, rows, levels), jnp.float32)
-    slots = -(-polar // parts)
+    kept_owner, lent_owner = share_rows(polar)
+    late = pltpu.VMEM((padded(rows - polar), levels), jnp.float32)
+    most = max(len(kept_owner), len(lent_owner))
+    some = len(lent_owner)
     dma = lambda *shape: pltpu.SemaphoreType.DMA(shape)
     swapped = lambda values: jnp.transpose(values, (1, 0, 2))
     result = pl.pallas_call(
-        functools.partial(block_kernel, rows, width, parts, bands, polar),
+        functools.partial(block_kernel, rows, width, parts, bands, polar, kept_owner, lent_owner),
         out_shape=jax.ShapeDtypeStruct((width, rows, levels), jnp.float32),
         in_specs=[pl.BlockSpec(memory_space=pltpu.SMEM)] + [hbm] * 7,
         out_specs=hbm,
@@ -574,11 +681,12 @@
             field(rows + 2), field(rows + 2), field(rows), field(rows), field(rows + 1), field(rows + 1),
             pltpu.VMEM(stack.shape, jnp.bfloat16),
             pltpu.VMEM(twist.shape, jnp.float32),
-            pltpu.VMEM((slots, parts, width, levels), jnp.float32),
+            field(parts),
             pltpu.VMEM((half, tall, 2 * levels), jnp.float32),
-            edge, edge, edge3, edge, edge, edge,
-            dma(5, rows), dma(2), dma(6), dma(6), dma(6), dma(6), dma(polar), dma(slots, parts),
-            dma(slots, parts), dma(polar), dma(rows),
+            field(some), field(some),
+            edge, edge, edge3, edge, edge, edge, late, late, late, late,
+            dma(5, rows), dma(2), dma(8), dma(8), dma(6), dma(6), dma(most), dma(parts),
+            dma(parts), dma(most), dma(some), dma(some), dma(some), dma(some), dma(rows),
         ],
         compiler_params=pltpu.CompilerParams(
             collective_id=0, has_side_effects=True, vmem_limit_bytes=60 * 2**20
@@ -599,10 +707,10 @@
         polar = tracer.shape[0] // 6
         rows = tracer.shape[0] // bands
         fits = (
-            bands > 2
-            and polar + SUBSTEPS <= rows
-            and parts <= polar <= parts + 2
-            and parts % 8 == 0
+            bands == 4
+            and polar + SUBSTEPS < rows
+            and 5 <= polar <= 13
+            and parts == 8
             and tracer.shape[2] == 128
         )
         body = functools.partial(on_block, mesh, polar) if fits else on_device

time: 106 us -> 102 us (0.962)
  Pallas kernels: 102 us -> 97.4 us
    pallas_call x1, Pallas kernels: 102 us -> 97.4 us  [on_block(): pl.pallas_call(functools.partial(block_kernel, rows, width, parts, bands,...]
where the time goes in v2:
time: 102 us
  Pallas kernels  97.4 us (95%)
  local copies, waits for them, and re-layouts  4.12 us (4%)
    pallas_call x1, Pallas kernels, on_block(): pl.pallas_call(functools.partial(block_kernel, rows, width, parts, bands,...  97.4 us
    unnamed x1, local copies, waits for them, and re-layouts  4.12 us

profile of v2, /device:TPU:7, one launch (start us, length us, event | category | flops | bytes accessed | tf_op | source)
XLA Modules:
  0.0 101.6 jit_solution(9976315685447776727)
XLA Ops:
  0.0 97.4 %shard_map.82 = f32[450,16,128]{2,1,0:T(8,128)} custom-call(s32[64]{0:T(128)} %cut_ref.1, f32[450,16,128]{2,1,0:T(8,128)} %bitcast.7, f32[450,16,128]{2,1,0:T(8,128)} %bitcast.8, f32[450,16,128]{2,1,0:T(8,128)} %bitcast.9, f32[450,16,128]{2,1,0:T(8,128)} %bitcast.10, f32[450,16,128]{2,1,0:T(8,128)} %bitcast.11, bf16[1856,464]{1,0:T(8,128)(2,1)} %constant.4.clone.dft_in, ...), custom_call_target="tpu_custom_call" | custom-call | tf_op jit(solution)/shard_map/pallas_call | solution.py:675
  97.4 4.1 %copy.10 = f32[16,450,128]{2,0,1:T(8,128)} copy(f32[16,450,128]{2,0,1:T(8,128)} %bitcast.6) | data formatting | bytes 7372800

commit v3 on v2

--- a/solution.py
+++ b/solution.py
@@ -178,7 +178,7 @@
 def block_kernel(
     rows, width, parts, bands, polar, kept_owner, lent_owner,
     cut_ref, f_in, ec_in, ed_in, sc_in, sd_in, dft_in, tw_in, out,
-    f0, f1, ec, ed, sc, sd, dft, tw, whole, spec, lent, lent_back,
+    f0, f1, ec, ed, sc, sd, dft, tw, whole, spec, lent, lent_back, land,
     to_east1, to_west1, from_west0, from_east0, from_west1, from_east1,
     to_east2, to_west2, from_west2, from_east2,
     load_sem, table_sem, lon_send, lon_recv, z_send, z_recv, go_send, go_recv, back_send, back_recv,
@@ -197,8 +197,9 @@
     pole_lat = jnp.where(ascending, 0, bands - 1)
     helper_lat = jnp.where(ascending, 1, bands - 2)
     early = polar + 1
-    tall = padded(width)
-    half = parts // 2 + 1
+    fold, sub = 2 * parts, width // 2
+    tall = padded(sub)
+    half = fold // 2 + 1
 
     def place(t):
         return jnp.where(ascending, t, rows - 1 - t)
@@ -402,35 +403,58 @@
             remote(
                 f0.at[1], whole.at[source], go_send.at[0], go_recv.at[source], {"lon": source}
             ).wait_recv()
-        extra = jnp.zeros((tall - width, 128), jnp.float32)
-        pieces = [whole[a] for a in range(parts)]
-        for q in range(half):
-            real, imag = None, None
-            for a in range(parts // 2):
-                merged = (
-                    pieces[a] + pieces[a + parts // 2] if q % 2 == 0 else pieces[a] - pieces[a + parts // 2]
+        def turned(index):
+            angle = 2.0 * math.pi * (index % fold) / fold
+            return math.cos(angle), math.sin(angle)
+
+        def weighted(terms):
+            total = None
+            for value, weight in terms:
+                if abs(weight) > 1e-9:
+                    term = value if abs(weight - 1.0) < 1e-9 else value * weight
+                    total = term if total is None else total + term
+            return total
+
+        quarter = fold // 4
+        chunks = [(start, min(48, sub - start)) for start in range(0, sub, 48)]
+        for start, size in chunks:
+            piece = [whole[a // 2, pl.ds((a % 2) * sub + start, size), :] for a in range(fold)]
+            sums = [piece[a] + piece[a + fold // 2] for a in range(fold // 2)]
+            diffs = [piece[a] - piece[a + fold // 2] for a in range(fold // 2)]
+            pairs = range(1, quarter)
+            even_real = [sums[a] + sums[fold // 2 - a] for a in pairs]
+            even_imag = [sums[a] - sums[fold // 2 - a] for a in pairs]
+            odd_real = [diffs[a] - diffs[fold // 2 - a] for a in pairs]
+            odd_imag = [diffs[a] + diffs[fold // 2 - a] for a in pairs]
+            space = (48 if start + 48 <= sub else tall - start) - size
+            for q in range(half):
+                first, cosines, sines = (
+                    (sums, even_real, even_imag) if q % 2 == 0 else (diffs, odd_real, odd_imag)
                 )
-                turn = 2.0 * math.pi * ((a * q) % parts) / parts
-                cosine, sine = math.cos(turn), math.sin(turn)
-                if abs(cosine) > 1e-9:
-                    term = merged if cosine > 1 - 1e-9 else merged * cosine
-                    real = term if real is None else real + term
-                if abs(sine) > 1e-9:
-                    term = merged * (-sine)
-                    imag = term if imag is None else imag + term
-            real = jnp.concatenate([real, extra], axis=0)
-            if imag is None:
-                new_real = real * tw[0, q]
-                new_imag = -real * tw[1, q]
-            else:
-                imag = jnp.concatenate([imag, extra], axis=0)
-                new_real = real * tw[0, q] + imag * tw[1, q]
-                new_imag = imag * tw[0, q] - real * tw[1, q]
-            spec[q, :, 0:128] = new_real
-            spec[q, :, 128:256] = new_imag
+                real = weighted(
+                    [(first[0], 1.0), (first[quarter], turned(quarter * q)[0])]
+                    + [(cosines[a - 1], turned(a * q)[0]) for a in pairs]
+                )
+                imag = weighted(
+                    [(first[quarter], -turned(quarter * q)[1])]
+                    + [(sines[a - 1], -turned(a * q)[1]) for a in pairs]
+                )
+                here = pl.ds(start, size)
+                by_cos, by_sin = tw[0, q, here, :], tw[1, q, here, :]
+                if imag is None:
+                    new_real, new_imag = real * by_cos, -real * by_sin
+                else:
+                    new_real = real * by_cos + imag * by_sin
+                    new_imag = imag * by_cos - real * by_sin
+                if space:
+                    extra = jnp.zeros((space, 128), jnp.float32)
+                    new_real = jnp.concatenate([new_real, extra], axis=0)
+                    new_imag = jnp.concatenate([new_imag, extra], axis=0)
+                spec[q, pl.ds(start, size + space), 0:128] = new_real
+                spec[q, pl.ds(start, size + space), 128:256] = new_imag
 
         cut = cut_ref[pole_lat * rows + base + r].astype(jnp.float32)
-        length = parts * width
+        length = fold * sub
 
         def products(values):
             high = values.astype(jnp.bfloat16)
@@ -441,12 +465,12 @@
             by_sin = main[tall : 2 * tall] + (main[3 * tall : 4 * tall] + rest[tall : 2 * tall])
             return by_cos, by_sin
 
-        @pl.loop(0, half)
+        @pl.loop(0, half, unroll=3)
         def _(q):
             by_cos, by_sin = products(spec[q])
             real = by_cos[:, 0:128] + by_sin[:, 128:256]
             imag = by_cos[:, 128:256] - by_sin[:, 0:128]
-            wave = q + parts * lax.broadcasted_iota(jnp.int32, (tall, 128), 0)
+            wave = q + fold * lax.broadcasted_iota(jnp.int32, (tall, 128), 0)
             folded = jnp.maximum(jnp.minimum(wave, length - wave), 1).astype(jnp.float32)
             ratio = cut / folded
             damping = jnp.minimum(1.0, ratio * ratio) * (1.0 / length)
@@ -457,17 +481,33 @@
             spec[q, :, 0:128] = real * tw[0, q] - imag * tw[1, q]
             spec[q, :, 128:256] = imag * tw[0, q] + real * tw[1, q]
 
-        for a in range(parts):
-            total = spec[0, 0:width, 0:128]
-            for q in range(1, half):
-                turn = 2.0 * math.pi * ((a * q) % parts) / parts
-                weight = 1.0 if q == parts // 2 else 2.0
-                cosine, sine = weight * math.cos(turn), weight * math.sin(turn)
-                if abs(cosine) > 1e-9:
-                    total = total + spec[q, 0:width, 0:128] * cosine
-                if abs(sine) > 1e-9:
-                    total = total - spec[q, 0:width, 128:256] * sine
-            whole[a] = total
+        for start, size in chunks:
+            here = pl.ds(start, size)
+            real = [spec[q, here, 0:128] * (1.0 if q in (0, half - 1) else 2.0) for q in range(half)]
+            imag = [spec[q, here, 128:256] * 2.0 for q in range(half)]
+
+            def collect(a, parity):
+                waves = [q for q in range(half) if q % 2 == parity]
+                in_cos = weighted([(real[q], turned(a * q)[0]) for q in waves])
+                in_sin = weighted(
+                    [(imag[q], turned(a * q)[1]) for q in waves if q not in (0, half - 1)]
+                )
+                zero = jnp.zeros((size, 128), jnp.float32)
+                return zero if in_cos is None else in_cos, zero if in_sin is None else in_sin
+
+            even, odd = [None] * (fold // 2), [None] * (fold // 2)
+            for a in range(quarter + 1):
+                in_cos, in_sin = collect(a, 0)
+                even[a] = in_cos - in_sin
+                odd_cos, odd_sin = collect(a, 1)
+                odd[a] = odd_cos - odd_sin
+                if 0 < a < quarter:
+                    even[fold // 2 - a] = in_cos + in_sin
+                    odd[fold // 2 - a] = -odd_cos - odd_sin
+            for a in range(fold // 2):
+                whole[a // 2, pl.ds((a % 2) * sub + start, size), :] = even[a] + odd[a]
+                other = a + fold // 2
+                whole[other // 2, pl.ds((other % 2) * sub + start, size), :] = even[a] - odd[a]
 
     def run_owner(owners, index_of, row_of, landing):
         for index, owner in enumerate(owners):
@@ -527,12 +567,15 @@
 
     def give_back(m):
         return remote(
-            lent_back.at[m], out.at[:, base + kept + m, :], ret_send.at[m], ret_recv.at[m],
+            lent_back.at[m], land.at[kept + m], ret_send.at[m], ret_recv.at[m],
             {"lat": pole_lat},
         )
 
     def kept_landing(r):
-        return out.at[:, base + r, :]
+        return land.at[r]
+
+    def store_row(r):
+        return pltpu.make_async_copy(land.at[r], out.at[:, base + r, :], out_sem.at[base + r])
 
     def lent_landing(m):
         return lent_back.at[m]
@@ -572,21 +615,33 @@
             load.wait()
         run_owner(kept_owner, inverse(kept_owner), lambda r: r, kept_landing)
 
+        @pl.loop(0, kept)
+        def _(r):
+            wait_back(r, pick(kept_owner, r), kept_landing)
+            store_row(r).start()
+
+        @pl.loop(0, borrowed)
+        def _(m):
+            give_back(m).wait_recv()
+            store_row(kept + m).start()
+
+        @pl.loop(0, kept)
+        def _(r):
+            wait_sent(r, pick(kept_owner, r), f0.at[1])
+
+        finish_owner(kept_owner, kept_landing)
+
+        @pl.loop(0, borrowed)
+        def _(m):
+            lend(m).wait_send()
+
         @pl.loop(polar, rows)
         def _(t):
             keep_row(place(t)).wait()
 
-        @pl.loop(0, kept)
+        @pl.loop(0, polar)
         def _(r):
-            wait_sent(r, pick(kept_owner, r), f0.at[1])
-            wait_back(r, pick(kept_owner, r), kept_landing)
-
-        finish_owner(kept_owner, kept_landing)
-
-        @pl.loop(0, borrowed)
-        def _(m):
-            lend(m).wait_send()
-            give_back(m).wait_recv()
+            store_row(r).wait()
 
     @pl.when(jnp.logical_not(is_polar))
     def _():
@@ -653,15 +708,15 @@
 
 
 def share_rows(polar):
-    lent = 2 * polar // 5
-    return (0, 7, 2, 4, 1, 6, 3, 5)[: polar - lent], (0, 2, 4, 6, 1, 3, 5, 7)[:lent]
+    lent = polar // 5
+    return tuple(range(polar - lent)), (0, 7, 2, 4)[:lent]
 
 
 def on_block(mesh, polar, tracer, east_courant, east_diffusion, south_courant, south_diffusion, cutoff):
     rows, width, levels = tracer.shape
     parts, bands = mesh.shape["lon"], mesh.shape["lat"]
-    tall, half = padded(width), parts // 2 + 1
-    stack, twist = tables(parts, width)
+    tall, half = padded(width // 2), parts + 1
+    stack, twist = tables(2 * parts, width // 2)
     hbm = pl.BlockSpec(memory_space=pl.ANY)
     field = lambda count: pltpu.VMEM((count, width, levels), jnp.float32)
     edge = pltpu.VMEM((rows, levels), jnp.float32)
@@ -683,7 +738,7 @@
             pltpu.VMEM(twist.shape, jnp.float32),
             field(parts),
             pltpu.VMEM((half, tall, 2 * levels), jnp.float32),
-            field(some), field(some),
+            field(some), field(some), field(polar),
             edge, edge, edge3, edge, edge, edge, late, late, late, late,
             dma(5, rows), dma(2), dma(8), dma(8), dma(6), dma(6), dma(most), dma(parts),
             dma(parts), dma(most), dma(some), dma(some), dma(some), dma(some), dma(rows),
@@ -709,7 +764,8 @@
         fits = (
             bands == 4
             and polar + SUBSTEPS < rows
-            and 5 <= polar <= 13
+            and 5 <= polar <= 10
+            and tracer.shape[1] % (2 * parts) == 0
             and parts == 8
             and tracer.shape[2] == 128
         )

time: 102 us -> 82.1 us (0.80)
  Pallas kernels: 97.4 us -> 77.8 us
    pallas_call x1, Pallas kernels: 97.4 us -> 77.8 us  [on_block(): pl.pallas_call(functools.partial(block_kernel, rows, width, parts, bands,...]
where the time goes in v3:
time: 82.1 us; the launch traced here: 82 us
  Pallas kernels  77.8 us (95%)
  local copies, waits for them, and re-layouts  4.12 us (5%)
    pallas_call x1, Pallas kernels, on_block(): pl.pallas_call(functools.partial(block_kernel, rows, width, parts, bands,...  77.8 us
    unnamed x1, local copies, waits for them, and re-layouts  4.12 us

profile of v3, /device:TPU:7, one launch (start us, length us, event | category | flops | bytes accessed | tf_op | source)
XLA Modules:
  0.0 82.0 jit_solution(3274055189283585433)
XLA Ops:
  0.0 77.8 %shard_map.82 = f32[450,16,128]{2,1,0:T(8,128)} custom-call(s32[64]{0:T(128)} %cut_ref.1, f32[450,16,128]{2,1,0:T(8,128)} %bitcast.7, f32[450,16,128]{2,1,0:T(8,128)} %bitcast.8, f32[450,16,128]{2,1,0:T(8,128)} %bitcast.9, f32[450,16,128]{2,1,0:T(8,128)} %bitcast.10, f32[450,16,128]{2,1,0:T(8,128)} %bitcast.11, bf16[960,240]{1,0:T(8,128)(2,1)} %constant.4.clone.dft_in, ...), custom_call_target="tpu_custom_call" | custom-call | tf_op jit(solution)/shard_map/pallas_call | solution.py:730
  77.9 4.1 %copy.10 = f32[16,450,128]{2,0,1:T(8,128)} copy(f32[16,450,128]{2,0,1:T(8,128)} %bitcast.6) | data formatting | bytes 7372800

commit v4 on v3

--- a/solution.py
+++ b/solution.py
@@ -303,17 +303,32 @@
         sd[rows] = nothing
 
     def advance_row(src, dst, j, edge, beyond):
-        value = src[j + 1]
-        beside = jnp.concatenate([value[1:], beyond], axis=0)
-        flux = ec[j] * 0.5 * (value + beside) - ed[j] * (beside - value)
-        first = value[0:1]
-        entering = from_west0[1, pl.ds(j, 1), :] * 0.5 * (edge + first) - from_west0[2, pl.ds(j, 1), :] * (first - edge)
-        flux_west = jnp.concatenate([entering, flux[:-1]], axis=0)
-        below = src[j]
-        above = src[j + 2]
-        flux_south = sc[j] * 0.5 * (below + value) - sd[j] * (value - below)
-        flux_north = sc[j + 1] * 0.5 * (value + above) - sd[j + 1] * (above - value)
-        dst[j + 1] = value - (flux - flux_west) - (flux_north - flux_south)
+        for start in range(0, width, 48):
+            size = min(48, width - start)
+            here = pl.ds(start, size)
+            value = src[j + 1, here, :]
+            if start + size < width:
+                beside = src[j + 1, pl.ds(start + 1, size), :]
+            else:
+                beside = jnp.concatenate([src[j + 1, pl.ds(start + 1, size - 1), :], beyond], axis=0)
+            if start:
+                before = pl.ds(start - 1, size)
+                behind, speed_west, mix_west = src[j + 1, before, :], ec[j, before, :], ed[j, before, :]
+            else:
+                before = pl.ds(0, size - 1)
+                behind = jnp.concatenate([edge, src[j + 1, before, :]], axis=0)
+                speed_west = jnp.concatenate(
+                    [from_west0[1, pl.ds(j, 1), :], ec[j, before, :]], axis=0
+                )
+                mix_west = jnp.concatenate([from_west0[2, pl.ds(j, 1), :], ed[j, before, :]], axis=0)
+            below, above = src[j, here, :], src[j + 2, here, :]
+            carried = (ec[j, here, :] * (value + beside) - speed_west * (behind + value)) + (
+                sc[j + 1, here, :] * (value + above) - sc[j, here, :] * (below + value)
+            )
+            mixed = (ed[j, here, :] * (beside - value) - mix_west * (value - behind)) + (
+                sd[j + 1, here, :] * (above - value) - sd[j, here, :] * (value - below)
+            )
+            dst[j + 1, here, :] = value + (mixed - 0.5 * carried)
 
     def wait_z0():
         @pl.when(has_south)
@@ -669,12 +684,12 @@
                     lend(m).wait_recv()
                     send_piece(lent.at[m], m, lent_owner[m])
 
+        for load in table_loads:
+            load.wait()
+        run_owner(lent_owner, inverse(lent_owner), lambda m: kept + m, lent_landing)
         wait_z1(ascending)
         second_early(0)
         keep_row(place(0)).start()
-        for load in table_loads:
-            load.wait()
-        run_owner(lent_owner, inverse(lent_owner), lambda m: kept + m, lent_landing)
 
         @pl.loop(0, borrowed)
         def _(m):

time: 82.1 us -> 78.8 us (0.960)
  Pallas kernels: 77.8 us -> 74.5 us
    pallas_call x1, Pallas kernels: 77.8 us -> 74.5 us  [on_block(): pl.pallas_call(functools.partial(block_kernel, rows, width, parts, bands,...]
where the time goes in v4:
time: 78.8 us; the launch traced here: 78.6 us
  Pallas kernels  74.5 us (95%)
  local copies, waits for them, and re-layouts  4.12 us (5%)
    pallas_call x1, Pallas kernels, on_block(): pl.pallas_call(functools.partial(block_kernel, rows, width, parts, bands,...  74.5 us
    unnamed x1, local copies, waits for them, and re-layouts  4.12 us

profile of v4, /device:TPU:7, one launch (start us, length us, event | category | flops | bytes accessed | tf_op | source)
XLA Modules:
  0.0 78.6 jit_solution(14808958167177173596)
XLA Ops:
  0.0 74.5 %shard_map.82 = f32[450,16,128]{2,1,0:T(8,128)} custom-call(s32[64]{0:T(128)} %cut_ref.1, f32[450,16,128]{2,1,0:T(8,128)} %bitcast.7, f32[450,16,128]{2,1,0:T(8,128)} %bitcast.8, f32[450,16,128]{2,1,0:T(8,128)} %bitcast.9, f32[450,16,128]{2,1,0:T(8,128)} %bitcast.10, f32[450,16,128]{2,1,0:T(8,128)} %bitcast.11, bf16[960,240]{1,0:T(8,128)(2,1)} %constant.4.clone.dft_in, ...), custom_call_target="tpu_custom_call" | custom-call | tf_op jit(solution)/shard_map/pallas_call | solution.py:745
  74.5 4.1 %copy.10 = f32[16,450,128]{2,0,1:T(8,128)} copy(f32[16,450,128]{2,0,1:T(8,128)} %bitcast.6) | data formatting | bytes 7372800

commit v5 on v4

--- a/solution.py
+++ b/solution.py
@@ -179,10 +179,9 @@
     rows, width, parts, bands, polar, kept_owner, lent_owner,
     cut_ref, f_in, ec_in, ed_in, sc_in, sd_in, dft_in, tw_in, out,
     f0, f1, ec, ed, sc, sd, dft, tw, whole, spec, lent, lent_back, land,
-    to_east1, to_west1, from_west0, from_east0, from_west1, from_east1,
-    to_east2, to_west2, from_west2, from_east2,
+    from_west0, from_east0, to_east1, to_west1, from_west1, from_east1,
     load_sem, table_sem, lon_send, lon_recv, z_send, z_recv, go_send, go_recv, back_send, back_recv,
-    lend_send, lend_recv, ret_send, ret_recv, out_sem,
+    lend_send, lend_recv, ret_send, ret_recv, out_sem, edge_send, edge_recv,
 ):
     me = lax.axis_index("lon")
     lat = lax.axis_index("lat")
@@ -196,7 +195,7 @@
     base = jnp.where(ascending, 0, rows - polar)
     pole_lat = jnp.where(ascending, 0, bands - 1)
     helper_lat = jnp.where(ascending, 1, bands - 2)
-    early = polar + 1
+    groups = rows // 4
     fold, sub = 2 * parts, width // 2
     tall = padded(sub)
     half = fold // 2 + 1
@@ -264,12 +263,11 @@
         remote(f_in.at[0], from_east0, lon_send.at[5], lon_recv.at[5], {"lon": west}),
     ]
     edges1 = [
-        remote(to_east1, from_west1, lon_send.at[2], lon_recv.at[2], {"lon": east}),
-        remote(to_west1, from_east1, lon_send.at[3], lon_recv.at[3], {"lon": west}),
-    ]
-    edges2 = [
-        remote(to_east2, from_west2, lon_send.at[6], lon_recv.at[6], {"lon": east}),
-        remote(to_west2, from_east2, lon_send.at[7], lon_recv.at[7], {"lon": west}),
+        (
+            remote(to_east1.at[g], from_west1.at[g], edge_send.at[0, g], edge_recv.at[0, g], {"lon": east}),
+            remote(to_west1.at[g], from_east1.at[g], edge_send.at[1, g], edge_recv.at[1, g], {"lon": west}),
+        )
+        for g in range(groups)
     ]
 
     for copy in edges0:
@@ -356,8 +354,8 @@
     for copy in edges0:
         copy.wait_recv()
 
-    def first_substep(start, stop, east_edge, west_edge):
-        @pl.loop(start, stop)
+    def first_group(group):
+        @pl.loop(4 * group, 4 * group + 4)
         def _(t):
             j = place(t)
 
@@ -367,14 +365,17 @@
                     load.wait()
 
             advance_row(f0, f1, j, from_west0[0, pl.ds(j, 1), :], from_east0[pl.ds(j, 1), :])
-            east_edge[pl.ds(t - start, 1), :] = f1[j + 1, width - 1 : width, :]
-            west_edge[pl.ds(t - start, 1), :] = f1[j + 1, 0:1, :]
-
-    def finish_first():
-        first_substep(early, rows, to_east2, to_west2)
-        for copy in edges2:
+            to_east1[group, pl.ds(t - 4 * group, 1), :] = f1[j + 1, width - 1 : width, :]
+            to_west1[group, pl.ds(t - 4 * group, 1), :] = f1[j + 1, 0:1, :]
+
+        for copy in edges1[group]:
             copy.start()
 
+    def wait_group(group):
+        for copy in edges1[group]:
+            copy.wait_recv()
+
+    def send_z1():
         @pl.when(has_north)
         def _():
             up1.start()
@@ -383,16 +384,9 @@
         def _():
             down1.start()
 
-    def second_early(t):
-        advance_row(f1, f0, place(t), from_west1[pl.ds(t, 1), :], from_east1[pl.ds(t, 1), :])
-
-    def second_late(t):
-        late = t - early
-        advance_row(f1, f0, place(t), from_west2[pl.ds(late, 1), :], from_east2[pl.ds(late, 1), :])
-
-    first_substep(0, early, to_east1, to_west1)
-    for copy in edges1:
-        copy.start()
+    def second(t):
+        group, spot = t // 4, pl.ds(t % 4, 1)
+        advance_row(f1, f0, place(t), from_west1[group, spot, :], from_east1[group, spot, :])
 
     def keep_row(j):
         return pltpu.make_async_copy(f0.at[j + 1], out.at[:, j, :], out_sem.at[j])
@@ -468,7 +462,7 @@
                 spec[q, pl.ds(start, size + space), 0:128] = new_real
                 spec[q, pl.ds(start, size + space), 128:256] = new_imag
 
-        cut = cut_ref[pole_lat * rows + base + r].astype(jnp.float32)
+        cut = cut_ref[pole_lat * rows + place(r)].astype(jnp.float32)
         length = fold * sub
 
         def products(values):
@@ -577,7 +571,7 @@
         return functools.partial(pick, table)
 
     def lend(m):
-        j = base + kept + m
+        j = place(m)
         return remote(f0.at[j + 1], lent.at[m], lend_send.at[m], lend_recv.at[m], {"lat": helper_lat})
 
     def give_back(m):
@@ -589,46 +583,58 @@
     def kept_landing(r):
         return land.at[r]
 
-    def store_row(r):
-        return pltpu.make_async_copy(land.at[r], out.at[:, base + r, :], out_sem.at[base + r])
+    def store_row(index):
+        j = place(jnp.where(index < kept, borrowed + index, index - kept))
+        return pltpu.make_async_copy(land.at[index], out.at[:, j, :], out_sem.at[j])
 
     def lent_landing(m):
         return lent_back.at[m]
 
     @pl.when(is_polar)
     def _():
-        for copy in edges1:
-            copy.wait_recv()
-
-        @pl.loop(0, polar)
-        def _(step):
-            r = jnp.where(step < borrowed, kept + step, lax.rem(me + step - borrowed, kept))
-            second_early(place(base + r))
-
-            @pl.when(step < borrowed)
-            def _():
-                lend(step).start()
-
-            @pl.when(step >= borrowed)
-            def _():
-                send_piece(f0.at[base + r + 1], r, pick(kept_owner, r))
-
+        def leave(start, stop):
+            count = stop - start
+
+            @pl.loop(0, count)
+            def _(step):
+                t = start + lax.rem(me // 2 + step, count) if start >= borrowed else start + step
+                second(t)
+
+                @pl.when(t < borrowed)
+                def _():
+                    lend(jnp.minimum(t, borrowed - 1)).start()
+
+                @pl.when(t >= borrowed)
+                def _():
+                    index = jnp.maximum(t - borrowed, 0)
+                    send_piece(f0.at[place(t) + 1], index, pick(kept_owner, index))
+
+        last = (polar + 3) // 4
+        for group in range(last):
+            first_group(group)
+            if group:
+                wait_group(group - 1)
+                leave(4 * group - 4, 4 * group)
+        wait_group(last - 1)
+        leave(4 * last - 4, polar)
         wait_z0()
-        finish_first()
-        second_early(polar)
-        keep_row(place(polar)).start()
+        for group in range(last, groups):
+            first_group(group)
+        send_z1()
+        for group in range(last, groups):
+            wait_group(group)
+
+        @pl.loop(polar, rows - 1)
+        def _(t):
+            second(t)
+            keep_row(place(t)).start()
+
         wait_z1(lat > 0)
-        for copy in edges2:
-            copy.wait_recv()
-
-        @pl.loop(early, rows)
-        def _(t):
-            second_late(t)
-            keep_row(place(t)).start()
-
+        second(rows - 1)
+        keep_row(place(rows - 1)).start()
         for load in table_loads:
             load.wait()
-        run_owner(kept_owner, inverse(kept_owner), lambda r: r, kept_landing)
+        run_owner(kept_owner, inverse(kept_owner), lambda r: borrowed + r, kept_landing)
 
         @pl.loop(0, kept)
         def _(r):
@@ -655,28 +661,23 @@
             keep_row(place(t)).wait()
 
         @pl.loop(0, polar)
-        def _(r):
-            store_row(r).wait()
+        def _(index):
+            store_row(index).wait()
 
     @pl.when(jnp.logical_not(is_polar))
     def _():
-        finish_first()
-        for copy in edges1 + edges2:
-            copy.wait_recv()
+        for group in range(groups):
+            first_group(group)
+        send_z1()
+        for group in range(groups):
+            wait_group(group)
         wait_z1(jnp.logical_not(ascending))
 
         @pl.loop(0, rows - 1)
         def _(step):
             t = rows - 1 - step
 
-            @pl.when(t >= early)
-            def _():
-                second_late(t)
-
-            @pl.when(t < early)
-            def _():
-                second_early(t)
-
+            second(t)
             keep_row(place(t)).start()
             for m in range(borrowed):
                 @pl.when(step == 5 + 3 * m)
@@ -686,9 +687,9 @@
 
         for load in table_loads:
             load.wait()
-        run_owner(lent_owner, inverse(lent_owner), lambda m: kept + m, lent_landing)
+        run_owner(lent_owner, inverse(lent_owner), lambda m: m, lent_landing)
         wait_z1(ascending)
-        second_early(0)
+        second(0)
         keep_row(place(0)).start()
 
         @pl.loop(0, borrowed)
@@ -707,7 +708,7 @@
 
         finish_owner(lent_owner, lent_landing)
 
-    for copy in edges0 + edges1 + edges2:
+    for copy in edges0 + [copy for pair in edges1 for copy in pair]:
         copy.wait_send()
 
     @pl.when(has_north)
@@ -724,7 +725,7 @@
 
 def share_rows(polar):
     lent = polar // 5
-    return tuple(range(polar - lent)), (0, 7, 2, 4)[:lent]
+    return (0, 2, 4, 6, 1, 3, 5, 7)[: polar - lent], (0, 7, 2, 4)[:lent]
 
 
 def on_block(mesh, polar, tracer, east_courant, east_diffusion, south_courant, south_diffusion, cutoff):
@@ -737,7 +738,7 @@
     edge = pltpu.VMEM((rows, levels), jnp.float32)
     edge3 = pltpu.VMEM((3, rows, levels), jnp.float32)
     kept_owner, lent_owner = share_rows(polar)
-    late = pltpu.VMEM((padded(rows - polar), levels), jnp.float32)
+    batch = pltpu.VMEM((rows // 4, 8, levels), jnp.float32)
     most = max(len(kept_owner), len(lent_owner))
     some = len(lent_owner)
     dma = lambda *shape: pltpu.SemaphoreType.DMA(shape)
@@ -754,9 +755,9 @@
             field(parts),
             pltpu.VMEM((half, tall, 2 * levels), jnp.float32),
             field(some), field(some), field(polar),
-            edge, edge, edge3, edge, edge, edge, late, late, late, late,
+            edge3, edge, batch, batch, batch, batch,
             dma(5, rows), dma(2), dma(8), dma(8), dma(6), dma(6), dma(most), dma(parts),
-            dma(parts), dma(most), dma(some), dma(some), dma(some), dma(some), dma(rows),
+            dma(parts), dma(most), dma(some), dma(some), dma(some), dma(some), dma(rows), dma(2, rows // 4), dma(2, rows // 4),
         ],
         compiler_params=pltpu.CompilerParams(
             collective_id=0, has_side_effects=True, vmem_limit_bytes=60 * 2**20
@@ -782,6 +783,8 @@
             and 5 <= polar <= 10
             and tracer.shape[1] % (2 * parts) == 0
             and parts == 8
+            and rows % 4 == 0
+            and -(-polar // 4) * 4 < rows
             and tracer.shape[2] == 128
         )
         body = functools.partial(on_block, mesh, polar) if fits else on_device

time: 78.8 us -> 78.8 us (level)
  no operation moved by 1% of the time
where the time goes in v5:
time: 78.8 us; the launch traced here: 78.6 us
  Pallas kernels  74.5 us (95%)
  local copies, waits for them, and re-layouts  4.12 us (5%)
    pallas_call x1, Pallas kernels, on_block(): pl.pallas_call(functools.partial(block_kernel, rows, width, parts, bands,...  74.5 us
    unnamed x1, local copies, waits for them, and re-layouts  4.12 us

profile of v5, /device:TPU:7, one launch (start us, length us, event | category | flops | bytes accessed | tf_op | source)
XLA Modules:
  0.0 78.6 jit_solution(3393737183844171022)
XLA Ops:
  0.0 74.5 %shard_map.82 = f32[450,16,128]{2,1,0:T(8,128)} custom-call(s32[64]{0:T(128)} %cut_ref.1, f32[450,16,128]{2,1,0:T(8,128)} %bitcast.7, f32[450,16,128]{2,1,0:T(8,128)} %bitcast.8, f32[450,16,128]{2,1,0:T(8,128)} %bitcast.9, f32[450,16,128]{2,1,0:T(8,128)} %bitcast.10, f32[450,16,128]{2,1,0:T(8,128)} %bitcast.11, bf16[960,240]{1,0:T(8,128)(2,1)} %constant.4.clone.dft_in, ...), custom_call_target="tpu_custom_call" | custom-call | tf_op jit(solution)/shard_map/pallas_call | solution.py:746
  74.5 4.1 %copy.10 = f32[16,450,128]{2,0,1:T(8,128)} copy(f32[16,450,128]{2,0,1:T(8,128)} %bitcast.6) | data formatting | bytes 7372800
